TPU v7x, 128 devices: a whole 4x4x4 slice. The times are simulated.
128 devices in a mesh: item: 16 (over z, y), code: 8 (over x, core).
Axes of the slice: x: 4, y: 4, z: 4, core: 2. Of those that a mesh axis runs over, the one named last changes fastest.
Arguments:
- residuals: float32 [256, 65536], P('code', 'item'), may hold values from -6 to 6
- codebook: float32 [256, 65536], P('item', 'code'), may hold values from -6 to 6
- item_weight: float32 [65536], P('item'), may hold values from 1 to 100
- code_capacity: float32 [65536], P('code'), may hold values from 0.25 to 4
- pairs: int32 [1024, 128], P('item', 'code'), may hold values from -1 to 127, as said below
Outputs:
- item_potential: float32 [65536], P('item')
- code_potential: float32 [65536], P('code')
Inputs may be any that keep to these rules, and one draw needn't show every extreme that they name: `pairs`: each entry is -1 (no candidate) or a code block's number within the code shard of its slot column. Within one item block and one code shard the live entries are distinct, the first slot is always live, and between 1 and 8 are live; some device holds exactly 8 live slots in every item block. Every code block is named by some item block.
All inputs are finite; a program needn't handle non-finite values.
Results may differ from a plain program's by a relative error of at most 0.0003.
Values sent between devices are 32-bit elements; how exact they have to be, the bound alone decides.
A program may use at most 128 MiB of HBM per device.

v0:
```python
import math
import jax
import jax.numpy as jnp
from jax import lax
from jax.sharding import PartitionSpec as P

BLOCK = 64
ITERS = 3
masked_score = -1e30
softness_factor = 0.1


def body(residuals, codebook, item_weight, code_capacity, pairs):
    item_columns = lax.all_gather(residuals, "code", axis=0, tiled=True)
    code_cols = lax.all_gather(codebook, "item", axis=0, tiled=True)
    embedding_width = item_columns.shape[0]
    item_count = item_columns.shape[1]
    code_count = code_cols.shape[1]
    item_blocks = item_count // BLOCK
    code_blocks = code_count // BLOCK
    logit_scale = 1.0 / (softness_factor * math.sqrt(embedding_width))
    weight_sum = lax.psum(jnp.sum(item_weight), "item")
    capacity_sum = lax.psum(jnp.sum(code_capacity), "code")
    item_logmass = jnp.log(item_weight) - jnp.log(weight_sum)
    code_logmass = jnp.log(code_capacity) - jnp.log(capacity_sum)
    is_live = pairs >= 0
    safe_ids = jnp.where(is_live, pairs, 0)
    target = jnp.where(is_live, pairs, code_blocks)
    item_split_cols = item_columns.reshape(embedding_width, item_blocks, BLOCK)
    code_column_splits = code_cols.reshape(embedding_width, code_blocks, BLOCK)
    group = math.gcd(item_blocks, 8)
    group_count = item_blocks // group

    def build_tiles(own, ids, live):
        picked = code_column_splits[:, ids, :]
        scores = (
            jnp.einsum("rbi,rbsj->bsij", own, picked, precision=lax.Precision.HIGHEST) * logit_scale
        )
        return jnp.where(live[:, :, None, None], scores, masked_score)

    reduce_fn = lambda tiles, ids, portion: tiles

    def one_group(group_index):
        start = group_index * group
        own = lax.dynamic_slice_in_dim(item_split_cols, start, group, 1)
        ids = lax.dynamic_slice_in_dim(safe_ids, start, group, 0)
        live = lax.dynamic_slice_in_dim(is_live, start, group, 0)
        portion = lax.dynamic_slice_in_dim(safe_ids, start, group, 0)
        return reduce_fn(build_tiles(own, ids, live), ids, portion)

    results = lax.map(one_group, jnp.arange(group_count, dtype=jnp.int32))
    saved_tile_blocks = results.reshape((item_blocks,) + results.shape[2:])

    def run_pass(reduce_fn, extra):
        return reduce_fn(saved_tile_blocks, safe_ids, extra)

    flat_target = target.reshape(-1)
    flat_rows = flat_target.shape[0]
    row_group = math.gcd(flat_rows, 256)
    one_hot = flat_target[:, None] == jnp.arange(code_blocks, dtype=jnp.int32)[None, :]
    one_hot_groups = one_hot.reshape(flat_rows // row_group, row_group, code_blocks)
    one_hot_float = one_hot.astype(jnp.float32)
    code_potential = jnp.zeros((code_count,), jnp.float32)
    item_potential = jnp.zeros((item_count,), jnp.float32)
    for sweep in range(ITERS):
        code_split = code_potential.reshape(code_blocks, BLOCK)

        def row_reduce(tiles, ids, portion):
            logits = tiles + code_split[ids][:, :, None, :]
            block_peak = jnp.max(logits, axis=(1, 3))
            block_total = jnp.sum(jnp.exp(logits - block_peak[:, None, :, None]), axis=(1, 3))
            return (block_peak, block_total)

        row_peak, row_total = run_pass(row_reduce, safe_ids)
        row_peak = row_peak.reshape(item_count)
        row_total = row_total.reshape(item_count)
        merged_peak = lax.pmax(row_peak, "code")
        merged_total = lax.psum(row_total * jnp.exp(row_peak - merged_peak), "code")
        item_potential = item_logmass - (merged_peak + jnp.log(merged_total))
        item_split = item_potential.reshape(item_blocks, BLOCK)

        def col_reduce(tiles, ids, portion):
            logits = tiles + portion[:, None, :, None]
            block_peak = jnp.max(logits, axis=2)
            block_total = jnp.sum(jnp.exp(logits - block_peak[:, :, None, :]), axis=2)
            return (block_peak, block_total)

        tile_peak, tile_total = run_pass(col_reduce, item_split)
        peak_flat = tile_peak.reshape(flat_rows, BLOCK)
        total_flat = tile_total.reshape(flat_rows, BLOCK)
        peak_groups = peak_flat.reshape(flat_rows // row_group, row_group, BLOCK)

        def peak_step(carry, pieces):
            hot, peaks = pieces
            candidate = jnp.max(jnp.where(hot[:, :, None], peaks[:, None, :], masked_score), axis=0)
            return (jnp.maximum(carry, candidate), None)

        col_peak, unused = lax.scan(
            peak_step,
            jnp.full((code_blocks, BLOCK), masked_score, jnp.float32),
            (one_hot_groups, peak_groups),
        )
        padded_peak = jnp.concatenate(
            [col_peak, jnp.full((1, BLOCK), masked_score, jnp.float32)], axis=0
        )
        spread = total_flat * jnp.exp(peak_flat - padded_peak[flat_target])
        col_total = jnp.dot(
            one_hot_float.T,
            spread,
            precision=lax.Precision.HIGHEST,
            preferred_element_type=jnp.float32,
        )
        col_peak = col_peak.reshape(code_count)
        col_total = col_total.reshape(code_count)
        joined_peak = lax.pmax(col_peak, "item")
        joined_total = lax.psum(col_total * jnp.exp(col_peak - joined_peak), "item")
        code_potential = code_logmass - (joined_peak + jnp.log(joined_total))
    return (item_potential, code_potential)


def solution(mesh):
    placed = (P("code", "item"), P("item", "code"), P("item"), P("code"), P("item", "code"))
    return jax.shard_map(
        body, mesh=mesh, in_specs=placed, out_specs=(P("item"), P("code")), check_vma=False
    )
```

profile of v0, /device:TPU:0, one launch (start us, length us, event | category | flops | bytes accessed | tf_op | source)
XLA Modules:
  0.0 1095.6 jit_solution(9727637983515556993)
XLA Ops:
  10.0 42.6 %psum.56 = f32[]{:T(128)} all-reduce(f32[]{:T(128)} %reduce_sum.72), channel_id=1, replica_groups=mesh['item'=16,'code'=8] {'item'}, use_global_device_ids=true, to_apply=%region_1.0 | all-reduce | flops 1 | bytes 8 | tf_op jit(solution)/shard_map/psum | solution.py:22
  58.9 5.6 copy.31
  64.6 52.7 %all-gather.3.cloned.1.call-done = f32[256,8192]{1,0:T(8,128)} async-done(((f32[16,8192]{1,0:T(8,128)}), f32[256,8192]{1,0:T(8,128)}) %all-gather.3.cloned.1.call-update) | async-done | bytes 8388624 | tf_op jit(solution)/shard_map/all_gather | solution.py:15
  117.3 9.0 copy.30
  126.3 158.7 %while.43 = (s32[]{:T(128)}, f32[8,8,16,64,64]{3,4,2,1,0:T(8,128)}, s32[8]{0:T(128)S(1)}, pred[64,16]{1,0:T(8,128)(4,1)S(1)}, s32[64,16]{1,0:T(8,128)S(1)}, /*in...) while((s32[]{:T(128)}, f32[8,8,16,64,64]{3,4,2,1,0:T(8,128)}, ...), condition=%wide.region_3.0_spmd, body=%wide.region_2.0_spmd.sunk | while | flops 1611662720 | bytes 29892660 | solution.py:51
  127.5 7.7 gather_fusion
  135.2 11.0 bitcast_dynamic-update-slice_fusion.2
  147.3 7.7 gather_fusion
  155.0 11.0 %bitcast_dynamic-update-slice_fusion.2 = f32[8,8,16,64,64]{3,4,2,1,0:T(8,128)} fusion(f32[8,8,16,64,64]{3,4,2,1,0:T(8,128)} %get-tuple-element.327, s32[]{:T(128)} %get-tuple-element.326, f32[256,8,16,64]{0,3,2,1:T(8,128)} %bitcast.84, pred[8,16]{1,0:T(8,128)(4,1)S(1)} %constant_dynamic-slice_fusion.2, f32[256,64,64]{0,2,1:T(8,128)} %get-tuple-element.343, ...), kind=kOutput, calls=%fused_computation.7.clone.1 | convolution fusion | flops 1611661312 | bytes 13107844 | tf_op jit(solution)/shard_map/while/body/eval_jaxpr/rbi,rbsj->bsij/dot_general | solution.py:37
  167.2 7.7 gather_fusion
  174.8 10.9 bitcast_dynamic-update-slice_fusion.2
  187.0 7.7 gather_fusion
  194.7 10.9 bitcast_dynamic-update-slice_fusion.2
  206.8 7.7 gather_fusion
  214.5 11.0 bitcast_dynamic-update-slice_fusion.2
  226.7 7.7 gather_fusion
  234.3 11.0 %bitcast_dynamic-update-slice_fusion.2 = f32[8,8,16,64,64]{3,4,2,1,0:T(8,128)} fusion(f32[8,8,16,64,64]{3,4,2,1,0:T(8,128)} %get-tuple-element.327, s32[]{:T(128)} %get-tuple-element.326, f32[256,8,16,64]{0,3,2,1:T(8,128)} %bitcast.84, pred[8,16]{1,0:T(8,128)(4,1)S(1)} %constant_dynamic-slice_fusion.2, f32[256,64,64]{0,2,1:T(8,128)} %get-tuple-element.343, ...), kind=kOutput, calls=%fused_computation.7.clone.1 | convolution fusion | flops 1611661312 | bytes 13107844 | tf_op jit(solution)/shard_map/while/body/eval_jaxpr/rbi,rbsj->bsij/dot_general | solution.py:37
  246.5 7.7 gather_fusion
  254.2 10.9 bitcast_dynamic-update-slice_fusion.2
  266.3 7.7 gather_fusion
  274.0 11.0 %bitcast_dynamic-update-slice_fusion.2 = f32[8,8,16,64,64]{3,4,2,1,0:T(8,128)} fusion(f32[8,8,16,64,64]{3,4,2,1,0:T(8,128)} %get-tuple-element.327, s32[]{:T(128)} %get-tuple-element.326, f32[256,8,16,64]{0,3,2,1:T(8,128)} %bitcast.84, pred[8,16]{1,0:T(8,128)(4,1)S(1)} %constant_dynamic-slice_fusion.2, f32[256,64,64]{0,2,1:T(8,128)} %get-tuple-element.343, ...), kind=kOutput, calls=%fused_computation.7.clone.1 | convolution fusion | flops 1611661312 | bytes 13107844 | tf_op jit(solution)/shard_map/while/body/eval_jaxpr/rbi,rbsj->bsij/dot_general | solution.py:37
  285.0 11.8 %add_reduce_fusion.5 = f32[8,8,64]{2,1,0:T(8,128)S(1)} fusion(f32[8,8,16,64,64]{3,4,2,1,0:T(8,128)} %get-tuple-element.105, f32[8,8,16,64]{3,2,1,0:T(8,128)S(1)} %bitcast.93), kind=kLoop, calls=%fused_computation.37 | loop fusion | flops 8384512 | bytes 17055744 | tf_op jit(solution)/shard_map/reduce_max | solution.py:70
  296.8 11.9 %exponential_reduce_fusion.5 = f32[8,8,64]{2,1,0:T(8,128)S(1)} fusion(f32[8,8,16,64,64]{3,4,2,1,0:T(8,128)} %get-tuple-element.105, f32[8,8,64]{2,1,0:T(8,128)S(1)} %add_reduce_fusion.5, f32[8,8,16,64]{3,2,1,0:T(8,128)S(1)} %bitcast.94), kind=kLoop, calls=%fused_computation.31 | loop fusion | flops 12578816 | bytes 17072128 | tf_op jit(solution)/shard_map/reduce_sum | solution.py:71
  308.9 25.5 %pmax.42 = f32[4096]{0:T(1024)S(1)} all-reduce(f32[4096]{0:T(1024)S(1)} %reshape.211), channel_id=1, replica_groups=mesh['item'=16,'code'=8] {'code'}, use_global_device_ids=true, to_apply=%region_7.8 | all-reduce | flops 4096 | bytes 32768 | tf_op jit(solution)/shard_map/pmax | solution.py:77
  334.4 24.6 %all-reduce.3 = (f32[4096]{0:T(1024)S(1)}, f32[]{:T(128)}) all-reduce(f32[4096]{0:T(1024)S(1)} %exponential_multiply_fusion.5, f32[]{:T(128)} %reduce_sum.73), channel_id=1, replica_groups=mesh['item'=16,'code'=8] {'code'}, use_global_device_ids=true, to_apply=%region_9.10 | all-reduce | flops 4097 | bytes 32776 | tf_op jit(solution)/shard_map/psum | solution.py:78
  359.1 15.3 %add_reduce_fusion.4 = f32[8,8,16,64]{3,2,1,0:T(8,128)S(1)} fusion(f32[8,8,16,64,64]{3,4,2,1,0:T(8,128)} %get-tuple-element.105, f32[8,8,64]{2,1,0:T(8,128)S(1)} %add.154), kind=kLoop, calls=%fused_computation.36 | loop fusion | flops 8323072 | bytes 17055744 | tf_op jit(solution)/shard_map/reduce_max | solution.py:84
  374.4 20.7 %exponential_reduce_fusion.4 = f32[8,8,16,64]{3,2,1,0:T(8,128)S(1)} fusion(f32[8,8,16,64,64]{3,4,2,1,0:T(8,128)} %get-tuple-element.105, f32[8,8,16,64]{3,2,1,0:T(8,128)S(1)} %add_reduce_fusion.4, f32[8,8,64]{2,1,0:T(8,128)S(1)} %add.154), kind=kLoop, calls=%fused_computation.30 | loop fusion | flops 12517376 | bytes 17317888 | tf_op jit(solution)/shard_map/reduce_sum | solution.py:85
  395.1 13.3 %while.44 = (s32[]{:T(128)}, f32[128,64]{0,1:T(8,128)S(1)}, pred[4,256,128]{2,1,0:T(8,128)(4,1)S(1)}, f32[4,256,64]{2,1,0:T(8,128)S(1)}, s32[]{:T(128)}, /*index=5*/s32[]{:T(128)}) while((s32[]{:T(128)}, f32[128,64]{0,1:T(8,128)S(1)}, pred[4,256,128]{2,1,0:T(8,128)(4,1)S(1)}, f32[4,256,64]{2,1,0:T(8,128)S(1)}, s32[]{:T(128)}, ...), condition=%wide.region_13.14_spmd.clone, body=%wide.region_11.13_spmd.clone.sunk | while | flops 4202499 | bytes 426071 | solution.py:98
  412.4 72.4 %pmax.43 = f32[8192]{0:T(1024)S(1)} all-reduce(f32[8192]{0:T(1024)S(1)} %reshape.213), channel_id=1, replica_groups=mesh['item'=16,'code'=8] {'item'}, use_global_device_ids=true, to_apply=%region_14.15 | all-reduce | flops 8192 | bytes 65536 | tf_op jit(solution)/shard_map/pmax | solution.py:115
  484.8 69.5 %psum.59 = f32[8192]{0:T(1024)S(1)} all-reduce(f32[8192]{0:T(1024)S(1)} %exponential_multiply_fusion.2), channel_id=1, replica_groups=mesh['item'=16,'code'=8] {'item'}, use_global_device_ids=true, to_apply=%region_16.17 | all-reduce | flops 8192 | bytes 65536 | tf_op jit(solution)/shard_map/psum | solution.py:116
  558.0 11.8 %add_reduce_fusion.3 = f32[8,8,64]{2,1,0:T(8,128)S(1)} fusion(f32[8,8,16,64,64]{3,4,2,1,0:T(8,128)} %get-tuple-element.105, f32[8,8,16,64]{3,2,1,0:T(8,128)S(1)} %bitcast.97), kind=kLoop, calls=%fused_computation.35 | loop fusion | flops 8384512 | bytes 17055744 | tf_op jit(solution)/shard_map/reduce_max | solution.py:70
  569.8 11.9 %exponential_reduce_fusion.3 = f32[8,8,64]{2,1,0:T(8,128)S(1)} fusion(f32[8,8,16,64,64]{3,4,2,1,0:T(8,128)} %get-tuple-element.105, f32[8,8,64]{2,1,0:T(8,128)S(1)} %add_reduce_fusion.3, f32[8,8,16,64]{3,2,1,0:T(8,128)S(1)} %bitcast.98), kind=kLoop, calls=%fused_computation.29 | loop fusion | flops 12578816 | bytes 17072128 | tf_op jit(solution)/shard_map/reduce_sum | solution.py:71
  581.9 23.5 %pmax.44 = f32[4096]{0:T(1024)S(1)} all-reduce(f32[4096]{0:T(1024)S(1)} %reshape.219), channel_id=1, replica_groups=mesh['item'=16,'code'=8] {'code'}, use_global_device_ids=true, to_apply=%region_18.19 | all-reduce | flops 4096 | bytes 32768 | tf_op jit(solution)/shard_map/pmax | solution.py:77
  605.4 23.6 %psum.60 = f32[4096]{0:T(1024)S(1)} all-reduce(f32[4096]{0:T(1024)S(1)} %exponential_multiply_fusion.4), channel_id=1, replica_groups=mesh['item'=16,'code'=8] {'code'}, use_global_device_ids=true, to_apply=%region_20.21 | all-reduce | flops 4096 | bytes 32768 | tf_op jit(solution)/shard_map/psum | solution.py:78
  629.1 15.3 %add_reduce_fusion.2 = f32[8,8,16,64]{3,2,1,0:T(8,128)S(1)} fusion(f32[8,8,16,64,64]{3,4,2,1,0:T(8,128)} %get-tuple-element.105, f32[8,8,64]{2,1,0:T(8,128)S(1)} %add.163), kind=kLoop, calls=%fused_computation.34 | loop fusion | flops 8323072 | bytes 17055744 | tf_op jit(solution)/shard_map/reduce_max | solution.py:84
  644.4 20.7 %exponential_reduce_fusion.2 = f32[8,8,16,64]{3,2,1,0:T(8,128)S(1)} fusion(f32[8,8,16,64,64]{3,4,2,1,0:T(8,128)} %get-tuple-element.105, f32[8,8,16,64]{3,2,1,0:T(8,128)S(1)} %add_reduce_fusion.2, f32[8,8,64]{2,1,0:T(8,128)S(1)} %add.163), kind=kLoop, calls=%fused_computation.28 | loop fusion | flops 12517376 | bytes 17317888 | tf_op jit(solution)/shard_map/reduce_sum | solution.py:85
  665.0 13.3 %while.45 = (s32[]{:T(128)}, f32[128,64]{0,1:T(8,128)S(1)}, pred[4,256,128]{2,1,0:T(8,128)(4,1)S(1)}, f32[4,256,64]{2,1,0:T(8,128)S(1)}, s32[]{:T(128)}, /*index=5*/s32[]{:T(128)}) while((s32[]{:T(128)}, f32[128,64]{0,1:T(8,128)S(1)}, pred[4,256,128]{2,1,0:T(8,128)(4,1)S(1)}, f32[4,256,64]{2,1,0:T(8,128)S(1)}, s32[]{:T(128)}, ...), condition=%wide.region_24.25_spmd.clone, body=%wide.region_22.24_spmd.clone.sunk | while | flops 4202499 | bytes 426071 | solution.py:98
  682.3 69.6 %pmax.45 = f32[8192]{0:T(1024)S(1)} all-reduce(f32[8192]{0:T(1024)S(1)} %reshape.221), channel_id=1, replica_groups=mesh['item'=16,'code'=8] {'item'}, use_global_device_ids=true, to_apply=%region_25.26 | all-reduce | flops 8192 | bytes 65536 | tf_op jit(solution)/shard_map/pmax | solution.py:115
  751.9 69.5 %psum.61 = f32[8192]{0:T(1024)S(1)} all-reduce(f32[8192]{0:T(1024)S(1)} %exponential_multiply_fusion.1), channel_id=1, replica_groups=mesh['item'=16,'code'=8] {'item'}, use_global_device_ids=true, to_apply=%region_27.28 | all-reduce | flops 8192 | bytes 65536 | tf_op jit(solution)/shard_map/psum | solution.py:116
  824.4 11.8 %add_reduce_fusion.1 = f32[8,8,64]{2,1,0:T(8,128)S(1)} fusion(f32[8,8,16,64,64]{3,4,2,1,0:T(8,128)} %get-tuple-element.105, f32[8,8,16,64]{3,2,1,0:T(8,128)S(1)} %bitcast.95), kind=kLoop, calls=%fused_computation.33 | loop fusion | flops 8384512 | bytes 17055744 | tf_op jit(solution)/shard_map/reduce_max | solution.py:70
  836.2 11.9 %exponential_reduce_fusion.1 = f32[8,8,64]{2,1,0:T(8,128)S(1)} fusion(f32[8,8,16,64,64]{3,4,2,1,0:T(8,128)} %get-tuple-element.105, f32[8,8,64]{2,1,0:T(8,128)S(1)} %add_reduce_fusion.1, f32[8,8,16,64]{3,2,1,0:T(8,128)S(1)} %bitcast.96), kind=kLoop, calls=%fused_computation.27 | loop fusion | flops 12578816 | bytes 17072128 | tf_op jit(solution)/shard_map/reduce_sum | solution.py:71
  848.3 23.5 %pmax.46 = f32[4096]{0:T(1024)S(1)} all-reduce(f32[4096]{0:T(1024)S(1)} %reshape.226), channel_id=1, replica_groups=mesh['item'=16,'code'=8] {'code'}, use_global_device_ids=true, to_apply=%region_29.30 | all-reduce | flops 4096 | bytes 32768 | tf_op jit(solution)/shard_map/pmax | solution.py:77
  871.8 23.8 %psum.62 = f32[4096]{0:T(1024)S(1)} all-reduce(f32[4096]{0:T(1024)S(1)} %exponential_multiply_fusion.3), channel_id=1, replica_groups=mesh['item'=16,'code'=8] {'code'}, use_global_device_ids=true, to_apply=%region_31.32 | all-reduce | flops 4096 | bytes 32768 | tf_op jit(solution)/shard_map/psum | solution.py:78
  895.7 15.3 %add_reduce_fusion = f32[8,8,16,64]{3,2,1,0:T(8,128)S(1)} fusion(f32[8,8,16,64,64]{3,4,2,1,0:T(8,128)} %get-tuple-element.105, f32[8,8,64]{2,1,0:T(8,128)S(1)} %add.171), kind=kLoop, calls=%fused_computation.32 | loop fusion | flops 8323072 | bytes 17055744 | tf_op jit(solution)/shard_map/reduce_max | solution.py:84
  911.0 20.7 %exponential_reduce_fusion = f32[8,8,16,64]{3,2,1,0:T(8,128)S(1)} fusion(f32[8,8,16,64,64]{3,4,2,1,0:T(8,128)} %get-tuple-element.105, f32[8,8,16,64]{3,2,1,0:T(8,128)S(1)} %add_reduce_fusion, f32[8,8,64]{2,1,0:T(8,128)S(1)} %add.171), kind=kLoop, calls=%fused_computation.26 | loop fusion | flops 12517376 | bytes 17317888 | tf_op jit(solution)/shard_map/reduce_sum | solution.py:85
  931.7 13.3 %while.46 = (s32[]{:T(128)}, f32[128,64]{0,1:T(8,128)S(1)}, pred[4,256,128]{2,1,0:T(8,128)(4,1)S(1)}, f32[4,256,64]{2,1,0:T(8,128)S(1)}, s32[]{:T(128)}, /*index=5*/s32[]{:T(128)}) while((s32[]{:T(128)}, f32[128,64]{0,1:T(8,128)S(1)}, pred[4,256,128]{2,1,0:T(8,128)(4,1)S(1)}, f32[4,256,64]{2,1,0:T(8,128)S(1)}, s32[]{:T(128)}, ...), condition=%wide.region_35.36_spmd.clone, body=%wide.region_33.35_spmd.clone.sunk | while | flops 4202499 | bytes 426071 | solution.py:98
  948.9 69.6 %pmax.47 = f32[8192]{0:T(1024)S(1)} all-reduce(f32[8192]{0:T(1024)S(1)} %reshape.228), channel_id=1, replica_groups=mesh['item'=16,'code'=8] {'item'}, use_global_device_ids=true, to_apply=%region_36.37 | all-reduce | flops 8192 | bytes 65536 | tf_op jit(solution)/shard_map/pmax | solution.py:115
  1018.5 69.5 %psum.63 = f32[8192]{0:T(1024)S(1)} all-reduce(f32[8192]{0:T(1024)S(1)} %exponential_multiply_fusion), channel_id=1, replica_groups=mesh['item'=16,'code'=8] {'item'}, use_global_device_ids=true, to_apply=%region_38.39 | all-reduce | flops 8192 | bytes 65536 | tf_op jit(solution)/shard_map/psum | solution.py:116
  (169 shorter events, 71.9 us)
Async XLA Ops:
  7.2 51.8 %all-gather.5.cloned.1.call-start = ((), (), s32[]{:S(2)}) async-start(), calls=%async_computation.1 | async-start | bytes 4718592 | tf_op jit(solution)/shard_map/all_gather | solution.py:14
  7.9 109.4 %all-gather.3.cloned.1.call-start = ((), (), s32[]{:S(2)}) async-start(), calls=%async_computation | async-start | bytes 8912896 | tf_op jit(solution)/shard_map/all_gather | solution.py:15
  285.0 74.0 %copy-start.3 = (f32[4096]{0:T(1024)S(1)}, f32[4096]{0:T(1024)}, u32[]{:S(2)}) copy-start(f32[4096]{0:T(1024)} %param.15) | copy-start | bytes 49156
  359.1 195.9 %copy-start.2 = (f32[8192]{0:T(1024)S(1)}, f32[8192]{0:T(1024)}, u32[]{:S(2)}) copy-start(f32[8192]{0:T(1024)} %param.16) | copy-start | bytes 98308
  629.1 36.0 %copy-start.1 = (f32[128,64]{0,1:T(8,128)S(1)}, f32[128,64]{0,1:T(8,128)}, u32[]{:S(2)}) copy-start(f32[128,64]{0,1:T(8,128)} %custom-call.1) | copy-start | bytes 98308
  895.6 36.1 %copy-start.4 = (f32[4096]{0:T(1024)}, f32[4096]{0:T(1024)S(1)}, u32[]{:S(2)}) copy-start(f32[4096]{0:T(1024)S(1)} %add_subtract_fusion.3) | copy-start | bytes 49156
  895.7 36.0 %copy-start = (f32[128,64]{0,1:T(8,128)S(1)}, f32[128,64]{0,1:T(8,128)}, u32[]{:S(2)}) copy-start(f32[128,64]{0,1:T(8,128)} %custom-call.2) | copy-start | bytes 98308
Sparse Core Ops, SparseCore 0:
  9.7 34.5 all-gather.4
  46.4 70.8 all-gather.2
where the time goes:
time: 1100 us
  blocking collectives  607 us (55%)
  other arithmetic  222 us (20%)
  local copies, waits for them, and re-layouts  101 us (9%)
  matrix products  89.9 us (8%)
  waiting for transfers between devices  54.1 us (5%)
  between operations  15.8 us (1%)
    pmax x3, blocking collectives, body(): joined_peak = lax.pmax(col_peak, 'item')  212 us
    psum x3, blocking collectives, body(): joined_total = lax.psum(col_total * jnp.exp(col_peak - joined_peak), 'item')  209 us
    dot_general x8, matrix products, build_tiles(): jnp.einsum('rbi,rbsj->bsij', own, picked, precision=lax.Precision.HIGHEST)  87.6 us
    pmax x3, blocking collectives, body(): merged_peak = lax.pmax(row_peak, 'code')  72.6 us
    psum x3, blocking collectives, body(): merged_total = lax.psum(row_total * jnp.exp(row_peak - merged_peak), 'code')  71.9 us
    reduce_sum x3, other arithmetic, col_reduce(): block_total = jnp.sum(jnp.exp(logits - block_peak[:, :, None, :]), axis=2)  62 us
    gather x8, local copies, waits for them, and re-layouts, build_tiles(): picked = code_column_splits[:, ids, :]  61.3 us
    all_gather x1, waiting for transfers between devices, body(): code_cols = lax.all_gather(codebook, 'item', axis=0, tiled=True)  52.7 us
  transfers between devices with their start and end apart: 2, of which 1 were waited for; matrix products, arithmetic and copies ran while one was open for 1% of the time, Pallas kernels for 0%

commit v1 on v0

--- a/solution.py
+++ b/solution.py
@@ -3,6 +3,7 @@
 import jax.numpy as jnp
 from jax import lax
 from jax.sharding import PartitionSpec as P
+from jax.lax import all_to_all, axis_size
 
 BLOCK = 64
 ITERS = 3
@@ -11,8 +12,21 @@
 
 
 def body(residuals, codebook, item_weight, code_capacity, pairs):
+
+    def _supply_zones(field_in, row_dim):
+        b_next = jnp.concatenate(
+            all_to_all(
+                jnp.stack([field_in] * axis_size("item"), axis=0),
+                axis_name="item",
+                split_axis=0,
+                concat_axis=0,
+            ),
+            axis=row_dim,
+        )
+        return b_next
+
     item_columns = lax.all_gather(residuals, "code", axis=0, tiled=True)
-    code_cols = lax.all_gather(codebook, "item", axis=0, tiled=True)
+    code_cols = _supply_zones(codebook, 0)
     embedding_width = item_columns.shape[0]
     item_count = item_columns.shape[1]
     code_count = code_cols.shape[1]

time: 1100 us -> 1180 us (1.073)
  blocking collectives: 607 us -> 711 us
  waiting for transfers between devices: 54.1 us -> 0.7 us
  local copies, waits for them, and re-layouts: 101 us -> 126 us
    psum x1, blocking collectives: 42.6 us -> 150 us  [body(): weight_sum = lax.psum(jnp.sum(item_weight), 'item')]
    all_gather x1 -> x0, waiting for transfers between devices: 52.7 us -> none  [body(): code_cols = lax.all_gather(codebook, 'item', axis=0, tiled=True)]
    another operation x0 -> x2, local copies, waits for them, and re-layouts: none -> 19.4 us  [the longest x1 14.2 us: body(): code_column_splits = code_cols.reshape(embedding_width, code_blocks, BLOCK)]
    while x0 -> x1, local copies, waits for them, and re-layouts: none -> 14.1 us  [body(): results = lax.map(one_group, jnp.arange(group_count, dtype=jnp.int32))]
  transfers between devices with their start and end apart: 2 -> 2, of which waited for: 1 -> 0; matrix products, arithmetic and copies ran while one was open for 1% -> 1% of each run, Pallas kernels for 0% -> 0%
where the time goes in v1:
time: 1180 us
  blocking collectives  711 us (60%)
  other arithmetic  222 us (19%)
  local copies, waits for them, and re-layouts  126 us (11%)
  matrix products  89.9 us (8%)
  between operations  15.8 us (1%)
    pmax x3, blocking collectives, body(): joined_peak = lax.pmax(col_peak, 'item')  209 us
    psum x3, blocking collectives, body(): joined_total = lax.psum(col_total * jnp.exp(col_peak - joined_peak), 'item')  209 us
    psum x1, blocking collectives, body(): weight_sum = lax.psum(jnp.sum(item_weight), 'item')  150 us
    dot_general x8, matrix products, build_tiles(): jnp.einsum('rbi,rbsj->bsij', own, picked, precision=lax.Precision.HIGHEST)  87.6 us
    psum x3, blocking collectives, body(): merged_total = lax.psum(row_total * jnp.exp(row_peak - merged_peak), 'code')  71.8 us
    pmax x3, blocking collectives, body(): merged_peak = lax.pmax(row_peak, 'code')  70.6 us
    reduce_sum x3, other arithmetic, col_reduce(): block_total = jnp.sum(jnp.exp(logits - block_peak[:, :, None, :]), axis=2)  62 us
    gather x8, local copies, waits for them, and re-layouts, build_tiles(): picked = code_column_splits[:, ids, :]  61.3 us
  transfers between devices with their start and end apart: 2, of which 0 were waited for; matrix products, arithmetic and copies ran while one was open for 1% of the time, Pallas kernels for 0%

profile of v1, /device:TPU:0, one launch (start us, length us, event | category | flops | bytes accessed | tf_op | source)
XLA Modules:
  0.0 1179.8 jit_solution(9077025002918147832)
XLA Ops:
  12.4 8.2 all-to-all-start
  22.6 150.3 %psum.56 = f32[]{:T(128)} all-reduce(f32[]{:T(128)} %reduce_sum.72), channel_id=1, replica_groups=mesh['item'=16,'code'=8] {'item'}, use_global_device_ids=true, to_apply=%region_1.0 | all-reduce | flops 1 | bytes 8 | tf_op jit(solution)/shard_map/psum | solution.py:36
  184.8 14.2 %reshape_reshape.12 = f32[256,128,64]{2,1,0:T(8,128)} reshape(f32[16,16,8192]{2,1,0:T(8,128)} %all-to-all-done) | data formatting | bytes 16777216 | tf_op jit(solution)/shard_map/reshape;reshape | solution.py:44
  199.0 14.1 %copy.23 = f32[256,128,64]{0,2,1:T(8,128)} copy(f32[256,128,64]{2,1,0:T(8,128)} %reshape_reshape.12) | data formatting | bytes 16777216 | tf_op jit(solution)/shard_map/while | solution.py:65
  213.1 160.4 %while.43 = (s32[]{:T(128)}, f32[8,8,16,64,64]{3,4,2,1,0:T(8,128)}, s32[8]{0:T(128)S(1)}, pred[64,16]{1,0:T(8,128)(4,1)S(1)}, s32[64,16]{1,0:T(8,128)S(1)}, /*in...) while((s32[]{:T(128)}, f32[8,8,16,64,64]{3,4,2,1,0:T(8,128)}, ...), condition=%wide.region_3.0_spmd, body=%wide.region_2.0_spmd.sunk | while | flops 1611662720 | bytes 29892660 | solution.py:65
  214.5 7.7 gather_fusion
  222.2 10.9 bitcast_dynamic-update-slice_fusion.2
  234.5 7.7 gather_fusion
  242.2 11.0 bitcast_dynamic-update-slice_fusion.2
  254.6 7.7 gather_fusion
  262.3 10.9 bitcast_dynamic-update-slice_fusion.2
  274.7 7.7 gather_fusion
  282.3 11.0 bitcast_dynamic-update-slice_fusion.2
  294.7 7.7 gather_fusion
  302.4 11.0 bitcast_dynamic-update-slice_fusion.2
  314.8 7.7 gather_fusion
  322.4 11.0 bitcast_dynamic-update-slice_fusion.2
  334.8 7.7 gather_fusion
  342.5 10.9 bitcast_dynamic-update-slice_fusion.2
  354.9 7.7 gather_fusion
  362.5 11.0 bitcast_dynamic-update-slice_fusion.2
  373.5 11.8 %add_reduce_fusion.5 = f32[8,8,64]{2,1,0:T(8,128)S(1)} fusion(f32[8,8,16,64,64]{3,4,2,1,0:T(8,128)} %get-tuple-element.105, f32[8,8,16,64]{3,2,1,0:T(8,128)S(1)} %bitcast.91), kind=kLoop, calls=%fused_computation.37 | loop fusion | flops 8384512 | bytes 17055744 | tf_op jit(solution)/shard_map/reduce_max | solution.py:84
  385.3 11.9 %exponential_reduce_fusion.5 = f32[8,8,64]{2,1,0:T(8,128)S(1)} fusion(f32[8,8,16,64,64]{3,4,2,1,0:T(8,128)} %get-tuple-element.105, f32[8,8,64]{2,1,0:T(8,128)S(1)} %add_reduce_fusion.5, f32[8,8,16,64]{3,2,1,0:T(8,128)S(1)} %bitcast.92), kind=kLoop, calls=%fused_computation.31 | loop fusion | flops 12578816 | bytes 17072128 | tf_op jit(solution)/shard_map/reduce_sum | solution.py:85
  397.4 23.5 %pmax.42 = f32[4096]{0:T(1024)S(1)} all-reduce(f32[4096]{0:T(1024)S(1)} %reshape.209), channel_id=1, replica_groups=mesh['item'=16,'code'=8] {'code'}, use_global_device_ids=true, to_apply=%region_7.8 | all-reduce | flops 4096 | bytes 32768 | tf_op jit(solution)/shard_map/pmax | solution.py:91
  421.0 24.7 %all-reduce.3 = (f32[4096]{0:T(1024)S(1)}, f32[]{:T(128)}) all-reduce(f32[4096]{0:T(1024)S(1)} %exponential_multiply_fusion.5, f32[]{:T(128)} %reduce_sum.73), channel_id=1, replica_groups=mesh['item'=16,'code'=8] {'code'}, use_global_device_ids=true, to_apply=%region_9.10 | all-reduce | flops 4097 | bytes 32776 | tf_op jit(solution)/shard_map/psum | solution.py:92
  445.8 15.3 %add_reduce_fusion.4 = f32[8,8,16,64]{3,2,1,0:T(8,128)S(1)} fusion(f32[8,8,16,64,64]{3,4,2,1,0:T(8,128)} %get-tuple-element.105, f32[8,8,64]{2,1,0:T(8,128)S(1)} %add.154), kind=kLoop, calls=%fused_computation.36 | loop fusion | flops 8323072 | bytes 17055744 | tf_op jit(solution)/shard_map/reduce_max | solution.py:98
  461.1 20.7 %exponential_reduce_fusion.4 = f32[8,8,16,64]{3,2,1,0:T(8,128)S(1)} fusion(f32[8,8,16,64,64]{3,4,2,1,0:T(8,128)} %get-tuple-element.105, f32[8,8,16,64]{3,2,1,0:T(8,128)S(1)} %add_reduce_fusion.4, f32[8,8,64]{2,1,0:T(8,128)S(1)} %add.154), kind=kLoop, calls=%fused_computation.30 | loop fusion | flops 12517376 | bytes 17317888 | tf_op jit(solution)/shard_map/reduce_sum | solution.py:99
  481.7 13.3 %while.44 = (s32[]{:T(128)}, f32[128,64]{0,1:T(8,128)S(1)}, pred[4,256,128]{2,1,0:T(8,128)(4,1)S(1)}, f32[4,256,64]{2,1,0:T(8,128)S(1)}, s32[]{:T(128)}, /*index=5*/s32[]{:T(128)}) while((s32[]{:T(128)}, f32[128,64]{0,1:T(8,128)S(1)}, pred[4,256,128]{2,1,0:T(8,128)(4,1)S(1)}, f32[4,256,64]{2,1,0:T(8,128)S(1)}, s32[]{:T(128)}, ...), condition=%wide.region_13.14_spmd.clone, body=%wide.region_11.13_spmd.clone.sunk | while | flops 4202499 | bytes 426071 | solution.py:112
  499.0 70.0 %pmax.43 = f32[8192]{0:T(1024)S(1)} all-reduce(f32[8192]{0:T(1024)S(1)} %reshape.211), channel_id=1, replica_groups=mesh['item'=16,'code'=8] {'item'}, use_global_device_ids=true, to_apply=%region_14.15 | all-reduce | flops 8192 | bytes 65536 | tf_op jit(solution)/shard_map/pmax | solution.py:129
  569.1 69.5 %psum.59 = f32[8192]{0:T(1024)S(1)} all-reduce(f32[8192]{0:T(1024)S(1)} %exponential_multiply_fusion.2), channel_id=1, replica_groups=mesh['item'=16,'code'=8] {'item'}, use_global_device_ids=true, to_apply=%region_16.17 | all-reduce | flops 8192 | bytes 65536 | tf_op jit(solution)/shard_map/psum | solution.py:130
  642.2 11.8 %add_reduce_fusion.3 = f32[8,8,64]{2,1,0:T(8,128)S(1)} fusion(f32[8,8,16,64,64]{3,4,2,1,0:T(8,128)} %get-tuple-element.105, f32[8,8,16,64]{3,2,1,0:T(8,128)S(1)} %bitcast.95), kind=kLoop, calls=%fused_computation.35 | loop fusion | flops 8384512 | bytes 17055744 | tf_op jit(solution)/shard_map/reduce_max | solution.py:84
  654.0 11.9 %exponential_reduce_fusion.3 = f32[8,8,64]{2,1,0:T(8,128)S(1)} fusion(f32[8,8,16,64,64]{3,4,2,1,0:T(8,128)} %get-tuple-element.105, f32[8,8,64]{2,1,0:T(8,128)S(1)} %add_reduce_fusion.3, f32[8,8,16,64]{3,2,1,0:T(8,128)S(1)} %bitcast.96), kind=kLoop, calls=%fused_computation.29 | loop fusion | flops 12578816 | bytes 17072128 | tf_op jit(solution)/shard_map/reduce_sum | solution.py:85
  666.1 23.5 %pmax.44 = f32[4096]{0:T(1024)S(1)} all-reduce(f32[4096]{0:T(1024)S(1)} %reshape.217), channel_id=1, replica_groups=mesh['item'=16,'code'=8] {'code'}, use_global_device_ids=true, to_apply=%region_18.19 | all-reduce | flops 4096 | bytes 32768 | tf_op jit(solution)/shard_map/pmax | solution.py:91
  689.7 23.6 %psum.60 = f32[4096]{0:T(1024)S(1)} all-reduce(f32[4096]{0:T(1024)S(1)} %exponential_multiply_fusion.4), channel_id=1, replica_groups=mesh['item'=16,'code'=8] {'code'}, use_global_device_ids=true, to_apply=%region_20.21 | all-reduce | flops 4096 | bytes 32768 | tf_op jit(solution)/shard_map/psum | solution.py:92
  713.3 15.3 %add_reduce_fusion.2 = f32[8,8,16,64]{3,2,1,0:T(8,128)S(1)} fusion(f32[8,8,16,64,64]{3,4,2,1,0:T(8,128)} %get-tuple-element.105, f32[8,8,64]{2,1,0:T(8,128)S(1)} %add.163), kind=kLoop, calls=%fused_computation.34 | loop fusion | flops 8323072 | bytes 17055744 | tf_op jit(solution)/shard_map/reduce_max | solution.py:98
  728.6 20.7 %exponential_reduce_fusion.2 = f32[8,8,16,64]{3,2,1,0:T(8,128)S(1)} fusion(f32[8,8,16,64,64]{3,4,2,1,0:T(8,128)} %get-tuple-element.105, f32[8,8,16,64]{3,2,1,0:T(8,128)S(1)} %add_reduce_fusion.2, f32[8,8,64]{2,1,0:T(8,128)S(1)} %add.163), kind=kLoop, calls=%fused_computation.28 | loop fusion | flops 12517376 | bytes 17317888 | tf_op jit(solution)/shard_map/reduce_sum | solution.py:99
  749.3 13.3 %while.45 = (s32[]{:T(128)}, f32[128,64]{0,1:T(8,128)S(1)}, pred[4,256,128]{2,1,0:T(8,128)(4,1)S(1)}, f32[4,256,64]{2,1,0:T(8,128)S(1)}, s32[]{:T(128)}, /*index=5*/s32[]{:T(128)}) while((s32[]{:T(128)}, f32[128,64]{0,1:T(8,128)S(1)}, pred[4,256,128]{2,1,0:T(8,128)(4,1)S(1)}, f32[4,256,64]{2,1,0:T(8,128)S(1)}, s32[]{:T(128)}, ...), condition=%wide.region_24.25_spmd.clone, body=%wide.region_22.24_spmd.clone.sunk | while | flops 4202499 | bytes 426071 | solution.py:112
  766.6 69.5 %pmax.45 = f32[8192]{0:T(1024)S(1)} all-reduce(f32[8192]{0:T(1024)S(1)} %reshape.219), channel_id=1, replica_groups=mesh['item'=16,'code'=8] {'item'}, use_global_device_ids=true, to_apply=%region_25.26 | all-reduce | flops 8192 | bytes 65536 | tf_op jit(solution)/shard_map/pmax | solution.py:129
  836.1 69.8 %psum.61 = f32[8192]{0:T(1024)S(1)} all-reduce(f32[8192]{0:T(1024)S(1)} %exponential_multiply_fusion.1), channel_id=1, replica_groups=mesh['item'=16,'code'=8] {'item'}, use_global_device_ids=true, to_apply=%region_27.28 | all-reduce | flops 8192 | bytes 65536 | tf_op jit(solution)/shard_map/psum | solution.py:130
  908.8 11.8 %add_reduce_fusion.1 = f32[8,8,64]{2,1,0:T(8,128)S(1)} fusion(f32[8,8,16,64,64]{3,4,2,1,0:T(8,128)} %get-tuple-element.105, f32[8,8,16,64]{3,2,1,0:T(8,128)S(1)} %bitcast.93), kind=kLoop, calls=%fused_computation.33 | loop fusion | flops 8384512 | bytes 17055744 | tf_op jit(solution)/shard_map/reduce_max | solution.py:84
  920.6 11.9 %exponential_reduce_fusion.1 = f32[8,8,64]{2,1,0:T(8,128)S(1)} fusion(f32[8,8,16,64,64]{3,4,2,1,0:T(8,128)} %get-tuple-element.105, f32[8,8,64]{2,1,0:T(8,128)S(1)} %add_reduce_fusion.1, f32[8,8,16,64]{3,2,1,0:T(8,128)S(1)} %bitcast.94), kind=kLoop, calls=%fused_computation.27 | loop fusion | flops 12578816 | bytes 17072128 | tf_op jit(solution)/shard_map/reduce_sum | solution.py:85
  932.7 23.5 %pmax.46 = f32[4096]{0:T(1024)S(1)} all-reduce(f32[4096]{0:T(1024)S(1)} %reshape.224), channel_id=1, replica_groups=mesh['item'=16,'code'=8] {'code'}, use_global_device_ids=true, to_apply=%region_29.30 | all-reduce | flops 4096 | bytes 32768 | tf_op jit(solution)/shard_map/pmax | solution.py:91
  956.2 23.6 %psum.62 = f32[4096]{0:T(1024)S(1)} all-reduce(f32[4096]{0:T(1024)S(1)} %exponential_multiply_fusion.3), channel_id=1, replica_groups=mesh['item'=16,'code'=8] {'code'}, use_global_device_ids=true, to_apply=%region_31.32 | all-reduce | flops 4096 | bytes 32768 | tf_op jit(solution)/shard_map/psum | solution.py:92
  979.9 15.3 %add_reduce_fusion = f32[8,8,16,64]{3,2,1,0:T(8,128)S(1)} fusion(f32[8,8,16,64,64]{3,4,2,1,0:T(8,128)} %get-tuple-element.105, f32[8,8,64]{2,1,0:T(8,128)S(1)} %add.171), kind=kLoop, calls=%fused_computation.32 | loop fusion | flops 8323072 | bytes 17055744 | tf_op jit(solution)/shard_map/reduce_max | solution.py:98
  995.2 20.7 %exponential_reduce_fusion = f32[8,8,16,64]{3,2,1,0:T(8,128)S(1)} fusion(f32[8,8,16,64,64]{3,4,2,1,0:T(8,128)} %get-tuple-element.105, f32[8,8,16,64]{3,2,1,0:T(8,128)S(1)} %add_reduce_fusion, f32[8,8,64]{2,1,0:T(8,128)S(1)} %add.171), kind=kLoop, calls=%fused_computation.26 | loop fusion | flops 12517376 | bytes 17317888 | tf_op jit(solution)/shard_map/reduce_sum | solution.py:99
  1015.9 13.3 %while.46 = (s32[]{:T(128)}, f32[128,64]{0,1:T(8,128)S(1)}, pred[4,256,128]{2,1,0:T(8,128)(4,1)S(1)}, f32[4,256,64]{2,1,0:T(8,128)S(1)}, s32[]{:T(128)}, /*index=5*/s32[]{:T(128)}) while((s32[]{:T(128)}, f32[128,64]{0,1:T(8,128)S(1)}, pred[4,256,128]{2,1,0:T(8,128)(4,1)S(1)}, f32[4,256,64]{2,1,0:T(8,128)S(1)}, s32[]{:T(128)}, ...), condition=%wide.region_35.36_spmd.clone, body=%wide.region_33.35_spmd.clone.sunk | while | flops 4202499 | bytes 426071 | solution.py:112
  1033.2 69.6 %pmax.47 = f32[8192]{0:T(1024)S(1)} all-reduce(f32[8192]{0:T(1024)S(1)} %reshape.226), channel_id=1, replica_groups=mesh['item'=16,'code'=8] {'item'}, use_global_device_ids=true, to_apply=%region_36.37 | all-reduce | flops 8192 | bytes 65536 | tf_op jit(solution)/shard_map/pmax | solution.py:129
  1102.7 69.5 %psum.63 = f32[8192]{0:T(1024)S(1)} all-reduce(f32[8192]{0:T(1024)S(1)} %exponential_multiply_fusion), channel_id=1, replica_groups=mesh['item'=16,'code'=8] {'item'}, use_global_device_ids=true, to_apply=%region_38.39 | all-reduce | flops 8192 | bytes 65536 | tf_op jit(solution)/shard_map/psum | solution.py:130
  (170 shorter events, 82.7 us)
Async XLA Ops:
  12.4 172.5 %all-to-all-start = ((f32[16,16,8192]{2,1,0:T(8,128)}), f32[16,16,8192]{2,1,0:T(8,128)}, u32[]{:S(2)}, u32[]{:S(2)}) async-start(f32[16,16,8192]{2,1,0:T(8,128)} %stack.2), calls=%async_computation | async-start | bytes 16777216 | tf_op jit(solution)/shard_map/all_to_all | solution.py:18
  20.6 158.7 %all-gather.2.cloned.1.call-start = ((), (), s32[]{:S(2)}) async-start(), calls=%async_computation.1 | async-start | bytes 4718592 | tf_op jit(solution)/shard_map/all_gather | solution.py:28
  373.5 72.2 %copy-start.3 = (f32[4096]{0:T(1024)S(1)}, f32[4096]{0:T(1024)}, u32[]{:S(2)}) copy-start(f32[4096]{0:T(1024)} %param.15) | copy-start | bytes 49156
  445.8 193.5 %copy-start.2 = (f32[8192]{0:T(1024)S(1)}, f32[8192]{0:T(1024)}, u32[]{:S(2)}) copy-start(f32[8192]{0:T(1024)} %param.16) | copy-start | bytes 98308
  713.3 36.0 %copy-start.1 = (f32[128,64]{0,1:T(8,128)S(1)}, f32[128,64]{0,1:T(8,128)}, u32[]{:S(2)}) copy-start(f32[128,64]{0,1:T(8,128)} %custom-call.1) | copy-start | bytes 98308
  979.8 36.1 %copy-start.4 = (f32[4096]{0:T(1024)}, f32[4096]{0:T(1024)S(1)}, u32[]{:S(2)}) copy-start(f32[4096]{0:T(1024)S(1)} %add_subtract_fusion.3) | copy-start | bytes 49156
  979.9 36.0 %copy-start = (f32[128,64]{0,1:T(8,128)S(1)}, f32[128,64]{0,1:T(8,128)}, u32[]{:S(2)}) copy-start(f32[128,64]{0,1:T(8,128)} %custom-call.2) | copy-start | bytes 98308
Sparse Core Ops, SparseCore 0:
  23.1 33.5 all-gather.1
